TPU v7x, 32 devices: a whole 2x2x4 slice. The times are simulated.
32 devices in a mesh: dp: 16 (over z, y, x), fsdp: 2 (over core).
Axes of the slice: x: 2, y: 2, z: 4, core: 2. Of those that a mesh axis runs over, the one named last changes fastest.
Arguments:
- tokens: bfloat16 [64, 256, 1024], P(('dp', 'fsdp')), may hold values from -6 to 6
- lengths: int32 [64], P(('dp', 'fsdp')), may hold values from 64 to 256, as said below
- cotangent: bfloat16 [64, 256, 1024], P(('dp', 'fsdp')), may hold values from -6 to 6
- query_weight: float32 [1024, 1024], P(('dp', 'fsdp')), may hold values from -0.25 to 0.25
- key_weight: float32 [1024, 1024], P(('dp', 'fsdp')), may hold values from -0.25 to 0.25
- value_weight: float32 [1024, 1024], P(('dp', 'fsdp')), may hold values from -0.1875 to 0.1875
- output_weight: float32 [1024, 1024], P(('dp', 'fsdp')), may hold values from -0.5 to 0.5
- query_bias: float32 [1024], P(('dp', 'fsdp')), may hold values from -3 to 3
- value_bias: float32 [1024], P(('dp', 'fsdp')), may hold values from -3 to 3
- output_bias: float32 [1024], P(('dp', 'fsdp')), may hold values from -3 to 3
- first_gain: float32 [1024], P(('dp', 'fsdp')), may hold values from 0.1 to 1.9
- first_shift: float32 [1024], P(('dp', 'fsdp')), may hold values from -3 to 3
- inner_weight: float32 [1024, 4096], P(('dp', 'fsdp')), may hold values from -0.1875 to 0.1875
- inner_bias: float32 [4096], P(('dp', 'fsdp')), may hold values from -3 to 3
- outer_weight: float32 [4096, 1024], P(('dp', 'fsdp')), may hold values from -0.09375 to 0.09375
- outer_bias: float32 [1024], P(('dp', 'fsdp')), may hold values from -3 to 3
- second_gain: float32 [1024], P(('dp', 'fsdp')), may hold values from 0.1 to 1.9
- second_shift: float32 [1024], P(('dp', 'fsdp')), may hold values from -3 to 3
Outputs:
- layer_out: bfloat16 [64, 256, 1024], P(('dp', 'fsdp'))
- tokens_gradient: bfloat16 [64, 256, 1024], P(('dp', 'fsdp'))
- query_weight_gradient: float32 [1024, 1024], P(('dp', 'fsdp'))
- key_weight_gradient: float32 [1024, 1024], P(('dp', 'fsdp'))
- value_weight_gradient: float32 [1024, 1024], P(('dp', 'fsdp'))
- output_weight_gradient: float32 [1024, 1024], P(('dp', 'fsdp'))
- query_bias_gradient: float32 [1024], P(('dp', 'fsdp'))
- value_bias_gradient: float32 [1024], P(('dp', 'fsdp'))
- output_bias_gradient: float32 [1024], P(('dp', 'fsdp'))
- first_gain_gradient: float32 [1024], P(('dp', 'fsdp'))
- first_shift_gradient: float32 [1024], P(('dp', 'fsdp'))
- inner_weight_gradient: float32 [1024, 4096], P(('dp', 'fsdp'))
- inner_bias_gradient: float32 [4096], P(('dp', 'fsdp'))
- outer_weight_gradient: float32 [4096, 1024], P(('dp', 'fsdp'))
- outer_bias_gradient: float32 [1024], P(('dp', 'fsdp'))
- second_gain_gradient: float32 [1024], P(('dp', 'fsdp'))
- second_shift_gradient: float32 [1024], P(('dp', 'fsdp'))
Inputs may be any that keep to these rules, and one draw needn't show every extreme that they name: `lengths`: in each aligned group of 2 sequences (those of one device) one, chosen by the seed, has length 256.
All inputs are finite; a program needn't handle non-finite values.
Results may differ from a plain program's by a relative error of at most 0.015.
The roundings to bfloat16 on the way count: a program that leaves them out, or rounds other values in their place, can miss the bound.
Values may be sent and summed in bfloat16 or wider, within the bound.
A program may use at most 256 MiB of HBM per device.

v0:
```python
import math

import jax
import jax.numpy as jnp
from jax import lax
from jax.sharding import PartitionSpec as P

HD = 64


epsilon = 1e-12


def normalize(hidden, gain, shift):
    center = hidden - jnp.mean(hidden, axis=-1, keepdims=True)
    spread = jnp.mean(center * center, axis=-1, keepdims=True)
    return center * lax.rsqrt(spread + epsilon) * gain + shift


def gelu_exact(inner):
    return jax.nn.gelu(inner, approximate=False)


def matmul(left, right):
    return jnp.dot(left, right, preferred_element_type=jnp.float32)


def matmul_left_t(left, right):
    return lax.dot_general(
        left, right, (((0,), (0,)), ((), ())), preferred_element_type=jnp.float32
    )


def matmul_right_t(left, right):
    return lax.dot_general(
        left, right, (((1,), (1,)), ((), ())), preferred_element_type=jnp.float32
    )


def row_sum(values):
    return jnp.sum(values.astype(jnp.float32), axis=0)


def per_device(
    tokens,
    lengths,
    cotangent,
    query_weight,
    key_weight,
    value_weight,
    output_weight,
    query_bias,
    value_bias,
    output_bias,
    first_gain,
    first_shift,
    inner_weight,
    inner_bias,
    outer_weight,
    outer_bias,
    second_gain,
    second_shift,
):
    attn_master = (
        query_weight,
        key_weight,
        value_weight,
        output_weight,
        query_bias,
        value_bias,
        output_bias,
        first_gain,
        first_shift,
    )
    ffn_master = (inner_weight, inner_bias, outer_weight, outer_bias, second_gain, second_shift)
    attn_half = [param.astype(jnp.bfloat16) for param in attn_master]
    ffn_half = [param.astype(jnp.bfloat16) for param in ffn_master]
    micro_count, rows, width = tokens.shape
    heads = width // HD
    owners = lax.axis_size(("dp", "fsdp"))
    scale = 1.0 / math.sqrt(HD)
    positions = jnp.arange(rows, dtype=jnp.int32)
    attn_totals = [
        jnp.zeros((param.shape[0] * owners,) + param.shape[1:], jnp.float32)
        for param in attn_master
    ]
    ffn_totals = [
        jnp.zeros((param.shape[0] * owners,) + param.shape[1:], jnp.float32) for param in ffn_master
    ]
    outputs_list = []
    token_grads_list = []
    for micro in range(micro_count):
        token_rows = tokens[micro]
        cot_rows = cotangent[micro].astype(jnp.float32)
        valid_keys = positions < lengths[micro]
        attn_full = (
            lax.all_gather(attn_half[0], ("dp", "fsdp"), axis=0, tiled=True),
            lax.all_gather(attn_half[1], ("dp", "fsdp"), axis=0, tiled=True),
            lax.all_gather(attn_half[2], ("dp", "fsdp"), axis=0, tiled=True),
            lax.all_gather(attn_half[3], ("dp", "fsdp"), axis=0, tiled=True),
            lax.all_gather(attn_half[4], ("dp", "fsdp"), axis=0, tiled=True),
            lax.all_gather(attn_half[5], ("dp", "fsdp"), axis=0, tiled=True),
            lax.all_gather(attn_half[6], ("dp", "fsdp"), axis=0, tiled=True),
            lax.all_gather(attn_half[7], ("dp", "fsdp"), axis=0, tiled=True),
            lax.all_gather(attn_half[8], ("dp", "fsdp"), axis=0, tiled=True),
        )
        query_use, key_use, value_use, output_use = (
            attn_full[0],
            attn_full[1],
            attn_full[2],
            attn_full[3],
        )
        bias_query = attn_full[4].astype(jnp.float32)
        bias_value = attn_full[5].astype(jnp.float32)
        bias_output = attn_full[6].astype(jnp.float32)
        gain_first = attn_full[7].astype(jnp.float32)
        shift_first = attn_full[8].astype(jnp.float32)
        query_rows = (matmul(token_rows, query_use) + bias_query).astype(jnp.bfloat16)
        key_rows = matmul(token_rows, key_use).astype(jnp.bfloat16)
        value_rows = (matmul(token_rows, value_use) + bias_value).astype(jnp.bfloat16)
        query_heads = query_rows.reshape(rows, heads, HD)
        key_heads = key_rows.reshape(rows, heads, HD)
        value_heads = value_rows.reshape(rows, heads, HD)

        def attention_scores():
            raw_scores = (
                jnp.einsum(
                    "qhd,khd->hqk", query_heads, key_heads, preferred_element_type=jnp.float32
                )
                * scale
            )
            return jnp.where(valid_keys[None, None, :], raw_scores, -1000000000.0)

        scores = attention_scores()
        peak = jnp.max(scores, axis=-1, keepdims=True)
        log_total = peak + jnp.log(jnp.sum(jnp.exp(scores - peak), axis=-1, keepdims=True))
        probs_low = jnp.exp(scores - log_total).astype(jnp.bfloat16)
        mixed = (
            jnp.einsum("hqk,khd->qhd", probs_low, value_heads, preferred_element_type=jnp.float32)
            .reshape(rows, width)
            .astype(jnp.bfloat16)
        )
        residual = token_rows.astype(jnp.float32) + matmul(mixed, output_use) + bias_output
        first = normalize(residual, gain_first, shift_first)
        first_low = first.astype(jnp.bfloat16)
        ffn_full = (
            lax.all_gather(ffn_half[0], ("dp", "fsdp"), axis=0, tiled=True),
            lax.all_gather(ffn_half[1], ("dp", "fsdp"), axis=0, tiled=True),
            lax.all_gather(ffn_half[2], ("dp", "fsdp"), axis=0, tiled=True),
            lax.all_gather(ffn_half[3], ("dp", "fsdp"), axis=0, tiled=True),
            lax.all_gather(ffn_half[4], ("dp", "fsdp"), axis=0, tiled=True),
            lax.all_gather(ffn_half[5], ("dp", "fsdp"), axis=0, tiled=True),
        )
        inner = matmul(first_low, ffn_full[0]) + ffn_full[1].astype(jnp.float32)
        active = gelu_exact(inner).astype(jnp.bfloat16)
        second_in = first + matmul(active, ffn_full[2]) + ffn_full[3].astype(jnp.float32)
        gain_second = ffn_full[4].astype(jnp.float32)
        shift_second = ffn_full[5].astype(jnp.float32)
        layer_rows, pull_second = jax.vjp(normalize, second_in, gain_second, shift_second)
        outputs_list.append(layer_rows.astype(jnp.bfloat16))
        ffn_full = (
            lax.all_gather(ffn_half[0], ("dp", "fsdp"), axis=0, tiled=True),
            lax.all_gather(ffn_half[1], ("dp", "fsdp"), axis=0, tiled=True),
            lax.all_gather(ffn_half[2], ("dp", "fsdp"), axis=0, tiled=True),
            lax.all_gather(ffn_half[3], ("dp", "fsdp"), axis=0, tiled=True),
            lax.all_gather(ffn_half[4], ("dp", "fsdp"), axis=0, tiled=True),
            lax.all_gather(ffn_half[5], ("dp", "fsdp"), axis=0, tiled=True),
        )
        d_second, d_gain_second, d_shift_second = pull_second(cot_rows)
        d_outer = d_second.astype(jnp.bfloat16)
        ffn_totals[2] = ffn_totals[2] + matmul_left_t(active, d_outer)
        ffn_totals[3] = ffn_totals[3] + row_sum(d_outer)
        ffn_totals[4] = ffn_totals[4] + d_gain_second
        ffn_totals[5] = ffn_totals[5] + d_shift_second
        d_active = matmul_right_t(d_outer, ffn_full[2])
        gelu_value, pull_gelu = jax.vjp(gelu_exact, inner)
        (d_inner,) = pull_gelu(d_active)
        d_inner_low = d_inner.astype(jnp.bfloat16)
        ffn_totals[0] = ffn_totals[0] + matmul_left_t(first_low, d_inner_low)
        ffn_totals[1] = ffn_totals[1] + row_sum(d_inner_low)
        d_first = matmul_right_t(d_inner_low, ffn_full[0]) + d_second
        attn_full = (
            lax.all_gather(attn_half[0], ("dp", "fsdp"), axis=0, tiled=True),
            lax.all_gather(attn_half[1], ("dp", "fsdp"), axis=0, tiled=True),
            lax.all_gather(attn_half[2], ("dp", "fsdp"), axis=0, tiled=True),
            lax.all_gather(attn_half[3], ("dp", "fsdp"), axis=0, tiled=True),
            lax.all_gather(attn_half[4], ("dp", "fsdp"), axis=0, tiled=True),
            lax.all_gather(attn_half[5], ("dp", "fsdp"), axis=0, tiled=True),
            lax.all_gather(attn_half[6], ("dp", "fsdp"), axis=0, tiled=True),
            lax.all_gather(attn_half[7], ("dp", "fsdp"), axis=0, tiled=True),
            lax.all_gather(attn_half[8], ("dp", "fsdp"), axis=0, tiled=True),
        )
        query_use, key_use, value_use, output_use = (
            attn_full[0],
            attn_full[1],
            attn_full[2],
            attn_full[3],
        )
        norm_value, pull_first = jax.vjp(
            normalize, residual, attn_full[7].astype(jnp.float32), attn_full[8].astype(jnp.float32)
        )
        d_residual, d_gain_first, d_shift_first = pull_first(d_first)
        attn_totals[7] = attn_totals[7] + d_gain_first
        attn_totals[8] = attn_totals[8] + d_shift_first
        d_branch = d_residual.astype(jnp.bfloat16)
        attn_totals[3] = attn_totals[3] + matmul_left_t(mixed, d_branch)
        attn_totals[6] = attn_totals[6] + row_sum(d_branch)
        d_mixed = matmul_right_t(d_branch, output_use).astype(jnp.bfloat16).reshape(rows, heads, HD)
        scores = attention_scores()
        probs = jnp.exp(scores - log_total)
        probs_low = probs.astype(jnp.bfloat16)
        d_probs = jnp.einsum(
            "qhd,khd->hqk", d_mixed, value_heads, preferred_element_type=jnp.float32
        )
        d_values = jnp.einsum(
            "hqk,qhd->khd", probs_low, d_mixed, preferred_element_type=jnp.float32
        ).reshape(rows, width)
        delta_rows = jnp.sum(probs * d_probs, axis=-1, keepdims=True)
        d_scores = (probs * (d_probs - delta_rows)).astype(jnp.bfloat16)
        d_queries = (
            (
                jnp.einsum("hqk,khd->qhd", d_scores, key_heads, preferred_element_type=jnp.float32)
                * scale
            )
            .reshape(rows, width)
            .astype(jnp.bfloat16)
        )
        d_keys = (
            jnp.einsum(
                "hqk,qhd->khd", d_scores, query_heads, preferred_element_type=jnp.float32
            ).reshape(rows, width)
            * scale
        )
        key_low = d_keys.astype(jnp.bfloat16)
        value_low = d_values.astype(jnp.bfloat16)
        attn_totals[0] = attn_totals[0] + matmul_left_t(token_rows, d_queries)
        attn_totals[1] = attn_totals[1] + matmul_left_t(token_rows, key_low)
        attn_totals[2] = attn_totals[2] + matmul_left_t(token_rows, value_low)
        attn_totals[4] = attn_totals[4] + row_sum(d_queries)
        attn_totals[5] = attn_totals[5] + row_sum(value_low)
        token_grad = (
            d_residual
            + matmul_right_t(d_queries, query_use)
            + matmul_right_t(key_low, key_use)
            + matmul_right_t(value_low, value_use)
        )
        token_grads_list.append(token_grad.astype(jnp.bfloat16))
    attn_shards = (
        lax.psum_scatter(attn_totals[0], ("dp", "fsdp"), scatter_dimension=0, tiled=True),
        lax.psum_scatter(attn_totals[1], ("dp", "fsdp"), scatter_dimension=0, tiled=True),
        lax.psum_scatter(attn_totals[2], ("dp", "fsdp"), scatter_dimension=0, tiled=True),
        lax.psum_scatter(attn_totals[3], ("dp", "fsdp"), scatter_dimension=0, tiled=True),
        lax.psum_scatter(attn_totals[4], ("dp", "fsdp"), scatter_dimension=0, tiled=True),
        lax.psum_scatter(attn_totals[5], ("dp", "fsdp"), scatter_dimension=0, tiled=True),
        lax.psum_scatter(attn_totals[6], ("dp", "fsdp"), scatter_dimension=0, tiled=True),
        lax.psum_scatter(attn_totals[7], ("dp", "fsdp"), scatter_dimension=0, tiled=True),
        lax.psum_scatter(attn_totals[8], ("dp", "fsdp"), scatter_dimension=0, tiled=True),
    )
    ffn_shards = (
        lax.psum_scatter(ffn_totals[0], ("dp", "fsdp"), scatter_dimension=0, tiled=True),
        lax.psum_scatter(ffn_totals[1], ("dp", "fsdp"), scatter_dimension=0, tiled=True),
        lax.psum_scatter(ffn_totals[2], ("dp", "fsdp"), scatter_dimension=0, tiled=True),
        lax.psum_scatter(ffn_totals[3], ("dp", "fsdp"), scatter_dimension=0, tiled=True),
        lax.psum_scatter(ffn_totals[4], ("dp", "fsdp"), scatter_dimension=0, tiled=True),
        lax.psum_scatter(ffn_totals[5], ("dp", "fsdp"), scatter_dimension=0, tiled=True),
    )
    return (
        jnp.stack(outputs_list),
        jnp.stack(token_grads_list),
        attn_shards[0],
        attn_shards[1],
        attn_shards[2],
        attn_shards[3],
        attn_shards[4],
        attn_shards[5],
        attn_shards[6],
        attn_shards[7],
        attn_shards[8],
        ffn_shards[0],
        ffn_shards[1],
        ffn_shards[2],
        ffn_shards[3],
        ffn_shards[4],
        ffn_shards[5],
    )


def solution(mesh):
    in_specs = (
        P(("dp", "fsdp"), None, None),
        P(("dp", "fsdp")),
        P(("dp", "fsdp"), None, None),
        P(("dp", "fsdp"), None),
        P(("dp", "fsdp"), None),
        P(("dp", "fsdp"), None),
        P(("dp", "fsdp"), None),
        P(("dp", "fsdp")),
        P(("dp", "fsdp")),
        P(("dp", "fsdp")),
        P(("dp", "fsdp")),
        P(("dp", "fsdp")),
        P(("dp", "fsdp"), None),
        P(("dp", "fsdp")),
        P(("dp", "fsdp"), None),
        P(("dp", "fsdp")),
        P(("dp", "fsdp")),
        P(("dp", "fsdp")),
    )
    out_specs = (
        P(("dp", "fsdp"), None, None),
        P(("dp", "fsdp"), None, None),
        P(("dp", "fsdp"), None),
        P(("dp", "fsdp"), None),
        P(("dp", "fsdp"), None),
        P(("dp", "fsdp"), None),
        P(("dp", "fsdp")),
        P(("dp", "fsdp")),
        P(("dp", "fsdp")),
        P(("dp", "fsdp")),
        P(("dp", "fsdp")),
        P(("dp", "fsdp"), None),
        P(("dp", "fsdp")),
        P(("dp", "fsdp"), None),
        P(("dp", "fsdp")),
        P(("dp", "fsdp")),
        P(("dp", "fsdp")),
    )
    return jax.shard_map(
        per_device, mesh=mesh, in_specs=in_specs, out_specs=out_specs, check_vma=False
    )
```

profile of v0, /device:TPU:0, one launch (start us, length us, event | category | flops | bytes accessed | tf_op | source)
XLA Modules:
  0.0 1444.9 jit_solution(9636509715736632032)
XLA Ops:
  7.2 1.6 convert_element_type.304
  8.9 1.5 convert_element_type.308
  13.8 1.8 convert_element_type.326
  15.6 1.8 convert_element_type.330
  24.4 42.4 %all-reduce.18 = (bf16[1024]{0:T(1024)(128)(2,1)S(1)}, bf16[1024]{0:T(1024)(128)(2,1)S(1)}, bf16[1024]{0:T(1024)(128)(2,1)S(1)}, bf16[1024]{0:T(1024)(128)(2,1)S...) all-reduce(bf16[1024]{0:T(1024)(128)(2,1)S(1)} %dynamic-update-slic, ...), channel_id=1, replica_groups=mesh['dp'=16,'fsdp'=2] {'dp','fsdp'}, use_global_device_ids=true, to_apply=%add | all-reduce | flops 8192 | bytes 32768
  68.0 40.4 %all-gather = bf16[32,1,128]{2,1,0:T(2,128)(2,1)S(1)} all-gather(bf16[1,1,128]{2,1,0:T(2,128)(2,1)S(1)} %convert_bitcast_fusion.2), channel_id=1, replica_groups=mesh['dp'=16,'fsdp'=2] {'dp','fsdp'}, dimensions={0}, use_global_device_ids=true | all-gather | bytes 8448 | tf_op jit(solution)/shard_map/all_gather | solution.py:148
  113.9 2.5 fusion.24
  117.4 12.0 all-gather.10.cloned.1.call-done
  129.4 2.3 fusion.25
  132.7 55.4 %all-gather.12.cloned.1.call-done = bf16[1024,1024]{1,0:T(8,128)(2,1)} async-done(((bf16[32,1024]{1,0:T(8,128)(2,1)}), bf16[1024,1024]{1,0:T(8,128)(2,1)}) %all-gather.12.cloned.1.call-update) | async-done | bytes 2097168 | tf_op jit(solution)/shard_map/all_gather | solution.py:98
  188.1 3.1 convolution_convert_fusion.7
  191.2 2.0 copy.83
  193.2 3.1 fusion.26
  196.3 2.0 copy.85
  201.2 2.5 convolution_convert_fusion.5
  207.8 2.6 convolution_convert_fusion.6
  210.4 36.2 %all-gather.14.cloned.1.call-done = bf16[1024,1024]{1,0:T(8,128)(2,1)} async-done(((bf16[32,1024]{1,0:T(8,128)(2,1)}), bf16[1024,1024]{1,0:T(8,128)(2,1)}) %all-gather.14.cloned.1.call-update) | async-done | bytes 2097168 | tf_op jit(solution)/shard_map/all_gather | solution.py:100
  246.6 2.6 fusion.95
  249.5 2.1 fusion.13
  257.0 68.7 %all-gather.16.cloned.1.call-done = bf16[1024,4096]{1,0:T(8,128)(2,1)} async-done(((bf16[32,4096]{1,0:T(8,128)(2,1)}), bf16[1024,4096]{1,0:T(8,128)(2,1)}) %all-gather.16.cloned.1.call-update) | async-done | bytes 8388624 | tf_op jit(solution)/shard_map/all_gather | solution.py:147
  325.7 16.1 %multiply_convert_fusion.3 = (bf16[256,4096]{1,0:T(8,128)(2,1)}, f32[256,4096]{1,0:T(8,128)}, f32[256,4096]{1,0:T(8,128)}) fusion(f32[4096]{0:T(1024)S(1)} %bitcast.228, bf16[1024,4096]{1,0:T(8,128)(2,1)} %all-gather.16.cloned.1.call-done, f32[256,1024]{1,0:T(8,128)S(1)} %get-tuple-element.138, f32[1024]{0:T(1024)S(1)} %convert_element_type.324, ...), kind=kOutput, calls=%fused_computation.35 | convolution fusion | flops 2218000384 | bytes 19949568 | tf_op jit(solution)/shard_map/dot_general | solution.py:25
  341.8 62.7 %all-gather.18.cloned.1.call-done = bf16[4096,1024]{1,0:T(8,128)(2,1)} async-done(((bf16[128,1024]{1,0:T(8,128)(2,1)}), bf16[4096,1024]{1,0:T(8,128)(2,1)}) %all-gather.18.cloned.1.call-update) | async-done | bytes 8388624 | tf_op jit(solution)/shard_map/all_gather | solution.py:149
  404.5 6.7 fusion.96
  411.4 13.4 multiply_convert_fusion.2
  424.9 2.5 fusion.98
  429.2 1.9 fusion.91
  432.6 11.8 convert_reduce_fusion
  444.4 6.8 convolution_add_fusion.17
  451.3 12.1 convert_reduce_fusion.1
  463.3 7.8 multiply_reduce_fusion.3
  471.2 1.6 fusion.88
  475.4 1.6 convolution_convert_fusion.1
  476.9 2.0 copy.93
  479.0 4.0 multiply_reduce_fusion
  483.0 2.5 multiply_convert_fusion
  485.6 2.9 convert_reduce_fusion.10
  490.1 1.6 convolution_convert_fusion.3
  491.7 2.1 copy.89
  493.8 4.2 multiply_reduce_fusion.1
  501.6 2.8 add_bitcast_fusion.2
  504.4 5.4 copy.108
  510.8 2.4 fusion.32
  513.2 2.6 fusion.29
  516.7 2.7 add_bitcast_fusion.1
  519.4 5.5 copy.110
  525.9 4.0 convert_reduce_fusion.9
  530.6 1.9 fusion.54
  535.2 2.6 add_bitcast_fusion
  537.8 5.4 copy.112
  544.3 1.8 fusion.99
  546.1 2.7 convolution_add_fusion.4
  549.4 4.1 fusion.81
  553.6 9.9 convolution_add_fusion.1
  564.6 4.0 fusion.100
  568.6 9.2 convolution_add_fusion
  579.7 40.6 %all-reduce.17 = (f32[1024]{0:T(1024)S(1)}, f32[1024]{0:T(1024)S(1)}, f32[1024]{0:T(1024)S(1)}, f32[1024]{0:T(1024)S(1)}, f32[1024]{0:T(1024)S(1)}, /*index=5*/f...) all-reduce(f32[1024]{0:T(1024)S(1)} %add.329, ...), channel_id=6, replica_groups=mesh['dp'=16,'fsdp'=2] {'dp','fsdp'}, use_global_device_ids=true, to_apply=%region_28.29.clone | all-reduce | flops 12288 | bytes 98304
  625.5 2.3 pad_maximum_fusion
  627.8 2.7 convolution_add_fusion.7
  635.9 13.9 reduce-scatter.19.cloned.1.call-done
  649.8 139.9 %reduce-scatter.21.cloned.1.call-done = f32[32,1024]{1,0:T(8,128)} async-done(((f32[1024,1024]{1,0:T(8,128)}), f32[32,1024]{1,0:T(8,128)}) %reduce-scatter.21.cloned.1.call-update) | async-done | bytes 131088
  789.7 139.7 %reduce-scatter.23.cloned.1.call-done = f32[32,1024]{1,0:T(8,128)} async-done(((f32[1024,1024]{1,0:T(8,128)}), f32[32,1024]{1,0:T(8,128)}) %reduce-scatter.23.cloned.1.call-update) | async-done | bytes 131088
  929.4 139.5 %reduce-scatter.13.cloned.1.call-done = f32[32,1024]{1,0:T(8,128)} async-done(((f32[1024,1024]{1,0:T(8,128)}), f32[32,1024]{1,0:T(8,128)}) %reduce-scatter.13.cloned.1.call-update) | async-done | bytes 131088 | tf_op jit(solution)/shard_map/reduce_scatter | solution.py:252
  1068.9 181.7 %reduce-scatter.15.cloned.1.call-done = f32[32,4096]{1,0:T(8,128)} async-done(((f32[1024,4096]{1,0:T(8,128)}), f32[32,4096]{1,0:T(8,128)}) %reduce-scatter.15.cloned.1.call-update) | async-done | bytes 524304 | tf_op jit(solution)/shard_map/reduce_scatter | solution.py:260
  1250.6 187.2 %reduce-scatter.17.cloned.1.call-done = f32[128,1024]{1,0:T(8,128)} async-done(((f32[4096,1024]{1,0:T(8,128)}), f32[128,1024]{1,0:T(8,128)}) %reduce-scatter.17.cloned.1.call-update) | async-done | bytes 524304 | tf_op jit(solution)/shard_map/reduce_scatter | solution.py:262
  (331 shorter events, 63.8 us)
Async XLA Ops:
  7.2 122.2 %copy-start.6 = (bf16[2,256,1024]{2,1,0:T(8,128)(2,1)S(1)}, bf16[2,256,1024]{2,1,0:T(8,128)(2,1)}, u32[]{:S(2)}) copy-start(bf16[2,256,1024]{2,1,0:T(8,128)(2,1)} %param.18) | copy-start | bytes 3145732
  7.2 106.7 %all-gather.8.cloned.1.call-start = ((), (), s32[]{:S(2)}) async-start(), calls=%async_computation.6 | async-start | bytes 2162688 | tf_op jit(solution)/shard_map/all_gather | solution.py:99
  8.9 120.5 %all-gather.10.cloned.1.call-start = ((), (), s32[]{:S(2)}) async-start(), calls=%async_computation.7 | async-start | bytes 2162688 | tf_op jit(solution)/shard_map/all_gather | solution.py:97
  10.5 177.6 %all-gather.12.cloned.1.call-start = ((), (), s32[]{:S(2)}) async-start(), calls=%async_computation.8 | async-start | bytes 2162688 | tf_op jit(solution)/shard_map/all_gather | solution.py:98
  12.1 234.5 %all-gather.14.cloned.1.call-start = ((), (), s32[]{:S(2)}) async-start(), calls=%async_computation.9 | async-start | bytes 2162688 | tf_op jit(solution)/shard_map/all_gather | solution.py:100
  13.7 311.9 %all-gather.16.cloned.1.call-start = ((), (), s32[]{:S(2)}) async-start(), calls=%async_computation.10 | async-start | bytes 8650752 | tf_op jit(solution)/shard_map/all_gather | solution.py:147
  15.6 388.9 %all-gather.18.cloned.1.call-start = ((), (), s32[]{:S(2)}) async-start(), calls=%async_computation.11 | async-start | bytes 8650752 | tf_op jit(solution)/shard_map/all_gather | solution.py:149
  17.4 632.4 %reduce-scatter.19.cloned.1.call-start = ((), (), s32[]{:S(2)}) async-start(), calls=%async_computation.15 | async-start | bytes 4325376
  112.7 93.1 %copy-start.88 = (pred[256]{0:T(512)(128)(4,1)}, pred[256]{0:T(512)(128)(4,1)S(1)}, u32[]{:S(2)}) copy-start(pred[256]{0:T(512)(128)(4,1)S(1)} %iota_compare_fusion.1) | copy-start | bytes 772
  132.7 65.7 %copy-start.17 = (bf16[1024,1024]{1,0:T(8,128)(2,1)S(1)}, bf16[1024,1024]{1,0:T(8,128)(2,1)}, u32[]{:S(2)}) copy-start(bf16[1024,1024]{1,0:T(8,128)(2,1)} %all-gather.10.cloned.1.call-done) | copy-start | bytes 6291460
  199.9 4.9 copy-start.33
  199.9 4.9 copy-start.36
  201.2 48.3 %copy-start.34 = (bf16[256,1024]{0,1:T(8,128)(2,1)}, bf16[256,1024]{0,1:T(8,128)(2,1)S(1)}, u32[]{:S(2)}) copy-start(bf16[256,1024]{0,1:T(8,128)(2,1)S(1)} %copy.86) | copy-start | bytes 1572868
  204.7 3.1 copy-start.45
  205.8 40.8 %copy-start.58 = (f32[1024]{0:T(1024)S(1)}, f32[1024]{0:T(1024)}, u32[]{:S(2)}) copy-start(f32[1024]{0:T(1024)} %convert_element_type.320) | copy-start | bytes 12292
  207.8 41.7 %copy-start.86 = (pred[256]{0:T(512)(128)(4,1)S(1)}, pred[256]{0:T(512)(128)(4,1)}, u32[]{:S(2)}) copy-start(pred[256]{0:T(512)(128)(4,1)} %iota_compare_fusion) | copy-start | bytes 772
  249.2 221.9 %copy-start.61 = (f32[256]{0:T(256)}, f32[256]{0:T(256)S(1)}, u32[]{:S(2)}) copy-start(f32[256]{0:T(256)S(1)} %broadcast_multiply_fusion.3) | copy-start | bytes 3076
  249.5 3.2 copy-start.46
  251.7 3.6 copy-start.19
  251.7 3.6 copy-start.59
  252.7 73.0 %copy-start.78 = (f32[32,1,128]{2,1,0:T(1,128)S(1)}, f32[32,1,128]{2,1,0:T(1,128)}, u32[]{:S(2)}) copy-start(f32[32,1,128]{2,1,0:T(1,128)} %convert_element_type.393) | copy-start | bytes 49156
  256.1 215.0 %copy-start.65 = (f32[256]{0:T(256)}, f32[256]{0:T(256)S(1)}, u32[]{:S(2)}) copy-start(f32[256]{0:T(256)S(1)} %broadcast_multiply_fusion.1) | copy-start | bytes 3076
  256.9 214.2 %copy-start.67 = (f32[256]{0:T(256)}, f32[256]{0:T(256)S(1)}, u32[]{:S(2)}) copy-start(f32[256]{0:T(256)S(1)} %fusion.75) | copy-start | bytes 3076
  256.9 214.2 %copy-start.79 = (f32[256]{0:T(256)}, f32[256]{0:T(256)S(1)}, u32[]{:S(2)}) copy-start(f32[256]{0:T(256)S(1)} %fusion.77) | copy-start | bytes 3076
  325.7 78.8 %copy-start.94 = (f32[1024]{0:T(1024)S(1)}, f32[1024]{0:T(1024)}, u32[]{:S(2)}) copy-start(f32[1024]{0:T(1024)} %convert_element_type.332) | copy-start | bytes 12292
  404.5 6.9 copy-start.95
  404.5 20.4 %slice-start = ((s8[8388608]{0:T(1024)(128)(4,1)}), s8[4194304]{0:T(1024)(128)(4,1)S(1)}, s32[]{:S(2)}) async-start(s8[8388608]{0:T(1024)(128)(4,1)} %bitcast.230), calls=%async_computation.18 | async-start | bytes 8388608
  411.4 13.5 slice-start.1
  424.8 2.6 copy-start.28
  424.9 2.9 copy-start.15
  424.9 2.9 copy-start.60
  431.8 12.6 copy-start.57
  432.6 18.7 %copy-start.49 = (bf16[256,1024]{1,0:T(8,128)(2,1)}, bf16[256,1024]{1,0:T(8,128)(2,1)S(1)}, u32[]{:S(2)}) copy-start(bf16[256,1024]{1,0:T(8,128)(2,1)S(1)} %get-tuple-element.102) | copy-start | bytes 1572868
  444.4 6.8 copy-start.42
  444.4 6.8 copy-start.96
  463.3 7.8 copy-start.56
  471.1 4.3 copy-start.20
  472.8 6.2 copy-start.87
  472.8 6.2 copy-start.81
  479.0 4.0 copy-start.3
  483.0 5.5 copy-start.11
  485.6 4.5 copy-start.21
  485.6 8.2 copy-start.89
  488.5 13.1 copy-start.30
  488.5 5.2 copy-start.83
  493.8 4.2 copy-start.1
  498.0 2.7 copy-start.8
  509.8 279.9 %reduce-scatter.21.cloned.1.call-start = ((), (), s32[]{:S(2)}) async-start(), calls=%async_computation.16 | async-start | bytes 4325376
  510.8 5.1 copy-start.9
  513.2 3.4 copy-start.31
  524.9 404.6 %reduce-scatter.23.cloned.1.call-start = ((), (), s32[]{:S(2)}) async-start(), calls=%async_computation.17 | async-start | bytes 4325376
  543.3 2.8 copy-start.44
  543.3 525.7 %reduce-scatter.13.cloned.1.call-start = ((), (), s32[]{:S(2)}) async-start(), calls=%async_computation.12 | async-start | bytes 4325376 | tf_op jit(solution)/shard_map/reduce_scatter | solution.py:252
  548.8 4.8 copy-start.66
  548.8 4.8 copy-start.80
  548.8 701.8 %reduce-scatter.15.cloned.1.call-start = ((), (), s32[]{:S(2)}) async-start(), calls=%async_computation.13 | async-start | bytes 17301504 | tf_op jit(solution)/shard_map/reduce_scatter | solution.py:260
  563.6 5.0 copy-start.29
  563.6 874.2 %reduce-scatter.17.cloned.1.call-start = ((), (), s32[]{:S(2)}) async-start(), calls=%async_computation.14 | async-start | bytes 17301504 | tf_op jit(solution)/shard_map/reduce_scatter | solution.py:262
  578.0 49.8 %copy-start.14 = (f32[256,1024]{1,0:T(8,128)S(1)}, f32[256,1024]{1,0:T(8,128)}, u32[]{:S(2)}) copy-start(f32[256,1024]{1,0:T(8,128)} %copy-done.13) | copy-start | bytes 3145732
  578.0 49.8 %copy-start.82 = (f32[256]{0:T(256)S(1)}, f32[256]{0:T(256)}, u32[]{:S(2)}) copy-start(f32[256]{0:T(256)} %copy-done.81) | copy-start | bytes 3076
  579.3 51.2 %copy-start.23 = (bf16[1024,1024]{1,0:T(8,128)(2,1)S(1)}, bf16[1024,1024]{1,0:T(8,128)(2,1)}, u32[]{:S(2)}) copy-start(bf16[1024,1024]{1,0:T(8,128)(2,1)} %all-gather.12.cloned.1.call-done) | copy-start | bytes 6291460
  620.2 10.2 copy-start.32
  627.8 3.5 copy-start.22
  627.8 3.5 copy-start.55
  (47 other events, 72.1 us)
Sparse Core Ops, SparseCore 0:
  11.5 59.1 all-gather.7
  74.1 55.2 all-gather.9
  132.8 55.2 all-gather.11
  191.4 55.2 all-gather.13
  249.3 76.2 all-gather.15
  328.4 76.0 all-gather.17
  509.9 139.8 reduce-scatter.18
  652.6 137.0 reduce-scatter.20
  792.6 136.8 reduce-scatter.22
  932.1 136.7 reduce-scatter.12
  1071.8 178.7 reduce-scatter.14
  1253.3 184.3 reduce-scatter.16
where the time goes:
time: 1450 us; the launch traced here: 1440 us
  waiting for transfers between devices  1040 us (72%)
  matrix products  178 us (12%)
  blocking collectives  123 us (8%)
  local copies, waits for them, and re-layouts  50.5 us (3%)
  other arithmetic  39.4 us (3%)
  between operations  15.7 us (1%)
    unnamed x15, waiting for transfers between devices  294 us
    reduce_scatter x1, waiting for transfers between devices, per_device(): lax.psum_scatter(ffn_totals[2], ('dp', 'fsdp'), scatter_dimension=0, tile...  187 us
    reduce_scatter x1, waiting for transfers between devices, per_device(): lax.psum_scatter(ffn_totals[0], ('dp', 'fsdp'), scatter_dimension=0, tile...  182 us
    reduce_scatter x1, waiting for transfers between devices, per_device(): lax.psum_scatter(attn_totals[3], ('dp', 'fsdp'), scatter_dimension=0, til...  139 us
    unnamed x2, blocking collectives  82.9 us
    all_gather x1, waiting for transfers between devices, per_device(): lax.all_gather(ffn_half[0], ('dp', 'fsdp'), axis=0, tiled=True)  68.7 us
    all_gather x1, waiting for transfers between devices, per_device(): lax.all_gather(ffn_half[2], ('dp', 'fsdp'), axis=0, tiled=True)  62.7 us
    dot_general x12, matrix products, matmul(): return jnp.dot(left, right, preferred_element_type=jnp.float32)  57.1 us
  transfers between devices with their start and end apart: 12, of which 11 were waited for; matrix products, arithmetic and copies ran while one was open for 10% of the time, Pallas kernels for 0%

commit v1 on v0

--- a/solution.py
+++ b/solution.py
@@ -1,15 +1,543 @@
+import functools
 import math
 
 import jax
 import jax.numpy as jnp
 from jax import lax
+from jax.experimental import pallas as pl
+from jax.experimental.pallas import tpu as pltpu
 from jax.sharding import PartitionSpec as P
 
+MESH = pl.DeviceIdType.MESH
+COPIES = 15
+
+
+class Place:
+    def __init__(self):
+        self.me = lax.axis_index("dp")
+        self.core = lax.axis_index("fsdp")
+        x, y, self.z = lax.rem(self.me, 2), lax.rem(self.me // 2, 2), self.me // 4
+        self.a = x + self.core * (y - x)
+        self.b = y + self.core * (x - y)
+        odd = lax.rem(self.z, 2)
+        self.pair, self.other = 3 - 2 * odd, 1 + 2 * odd
+        self.z_pair = self.z + 1 - 2 * odd
+
+    def chip(self, z, a, b):
+        return z * 4 + (b + self.core * (a - b)) * 2 + (a + self.core * (b - a))
+
+    def back(self, j):
+        return lax.rem(self.z - j + 4, 4)
+
+    def peers(self):
+        along_z = [self.chip(lax.rem(self.z + k, 4), self.a, self.b) for k in (1, 2, 3)]
+        return along_z + [self.chip(self.z, 1 - self.a, self.b), self.chip(self.z, self.a, 1 - self.b)]
+
+    def meet(self):
+        sem = pltpu.get_barrier_semaphore()
+        peers = self.peers()
+        for chip in peers:
+            pl.semaphore_signal(sem, inc=1, device_id=(chip, self.core), device_id_type=MESH)
+        pl.semaphore_signal(sem, inc=1, device_id=(self.me, 1 - self.core), device_id_type=MESH)
+        pl.semaphore_wait(sem, len(peers) + 1)
+
+
+class Hops:
+    def __init__(self, place, send_sem, recv_sem, base):
+        self.place, self.send_sem, self.recv_sem, self.base = place, send_sem, recv_sem, base
+        self.started = []
+
+    def send(self, k, source, target, chip):
+        copy = pltpu.make_async_remote_copy(
+            src_ref=source,
+            dst_ref=target,
+            send_sem=self.send_sem.at[self.base + k],
+            recv_sem=self.recv_sem.at[self.base + k],
+            device_id=(chip, self.place.core),
+            device_id_type=MESH,
+        )
+        copy.start()
+        self.started.append(copy)
+
+    def arrived(self, k, block):
+        pltpu.make_async_remote_copy(
+            src_ref=block,
+            dst_ref=block,
+            send_sem=self.send_sem.at[self.base + k],
+            recv_sem=self.recv_sem.at[self.base + k],
+            device_id=(self.place.me, self.place.core),
+            device_id_type=MESH,
+        ).wait_recv()
+
+    def finish(self):
+        for copy in self.started:
+            copy.wait_send()
+
+
+class Gather(Hops):
+    def __init__(self, place, held, *rest):
+        super().__init__(place, *rest)
+        self.held = held
+
+    def pass_on(self, k, block, chip):
+        self.send(k, self.held.at[block], self.held.at[block], chip)
+
+    def along_z(self, k):
+        p = self.place
+        self.pass_on(k - 1, p.me, p.chip(lax.rem(p.z + k, 4), p.a, p.b))
+
+    def along_a(self, j):
+        p = self.place
+        self.pass_on(3 + j, p.chip(p.back(j), p.a, p.b), p.chip(p.z, 1 - p.a, p.b))
+
+    def along_b(self, i):
+        p = self.place
+        j = (0, 0, 2, 2, p.other, p.other)[i]
+        a = (p.a, 1 - p.a)[i % 2]
+        self.pass_on(7 + i, p.chip(p.back(j), a, p.b), p.chip(p.z, p.a, 1 - p.b))
+
+    def to_pair(self, i):
+        p = self.place
+        a = (p.a, 1 - p.a)[i]
+        self.pass_on(13 + i, p.chip(p.z, a, 1 - p.b), p.chip(p.z_pair, p.a, p.b))
+
+    def wait(self, k):
+        self.arrived(k, self.held.at[self.place.me])
+
+    def step0(self):
+        self.along_z(2)
+        self.along_a(0)
+        self.along_b(0)
+        self.along_z(1)
+        self.along_z(3)
+
+    def step1(self):
+        p = self.place
+        self.wait(3)
+        self.along_b(1)
+        self.wait(7)
+        self.to_pair(0)
+        self.wait(1)
+        self.along_a(2)
+        self.along_b(2)
+        self.wait(p.other - 1)
+        self.along_a(p.other)
+        self.along_b(4)
+        self.wait(p.pair - 1)
+        self.along_a(p.pair)
+
+    def step2(self):
+        p = self.place
+        self.wait(8)
+        self.to_pair(1)
+        self.wait(5)
+        self.along_b(3)
+        self.wait(3 + p.other)
+        self.along_b(5)
+
+    def step3(self):
+        self.wait(3 + self.place.pair)
+        for k in (9, 10, 11, 12, 13, 14):
+            self.wait(k)
+
+
+class Reduce(Hops):
+    def __init__(self, place, terms, landed, *rest):
+        super().__init__(place, *rest)
+        self.terms, self.landed = terms, landed
+
+    def add(self, block, ks):
+        for k in ks:
+            self.arrived(k, self.landed.at[k])
+        total = self.terms[block].astype(jnp.float32)
+        for k in ks:
+            total += self.landed[k].astype(jnp.float32)
+        return total
+
+    def add_and_send(self, k, block, ks, chip):
+        if ks:
+            self.terms[block] = self.add(block, ks).astype(self.terms.dtype)
+        self.send(k, self.terms.at[block], self.landed.at[k], chip)
+
+    def to_pair(self, i):
+        p = self.place
+        a = (p.a, 1 - p.a)[i]
+        self.add_and_send(13 + i, p.chip(p.z_pair, a, 1 - p.b), (), p.chip(p.z_pair, p.a, p.b))
+
+    def along_b(self, i):
+        p = self.place
+        j = (0, 0, 2, 2, p.other, p.other)[i]
+        a = (p.a, 1 - p.a)[i % 2]
+        ks = (13 + i,) if i < 2 else ()
+        self.add_and_send(7 + i, p.chip(p.back(j), a, 1 - p.b), ks, p.chip(p.z, p.a, 1 - p.b))
+
+    def along_a(self, j, ks):
+        p = self.place
+        self.add_and_send(3 + j, p.chip(p.back(j), 1 - p.a, p.b), ks, p.chip(p.z, 1 - p.a, p.b))
+
+    def along_z(self, j, ks):
+        p = self.place
+        owner = p.chip(p.back(j), p.a, p.b)
+        self.add_and_send(3 - j, owner, ks, owner)
+
+    def step0(self):
+        self.to_pair(0)
+        self.to_pair(1)
+        for i in (3, 5, 2, 4):
+            self.along_b(i)
+        self.along_a(self.place.pair, ())
+
+    def step1(self):
+        self.along_b(1)
+        self.along_b(0)
+
+    def step2(self):
+        p = self.place
+        self.along_a(2, (10,))
+        self.along_a(p.other, (12,))
+        self.along_a(0, (8,))
+
+    def step3(self):
+        p = self.place
+        self.along_z(p.pair, (3 + p.pair,))
+        self.along_z(2, (9, 5))
+        self.along_z(p.other, (11, 3 + p.other))
+
+    def result(self):
+        return self.add(self.place.me, (7, 3, 0, 1, 2))
+
+
+ORDER = ((0, 0), (0, 1), (1, 0), (0, 2), (1, 1), (0, 3), (2, 0), (1, 2), (2, 1), (1, 3), (2, 2), (2, 3))
+
+
+def gather_kernel(
+    units, vecs, out_units, out_vecs, local_sem, core_send, core_recv, send_sem, recv_sem
+):
+    place = Place()
+    me, core = place.me, place.core
+    local = [
+        pltpu.make_async_copy(units.at[u], out_units.at[u, core, me], local_sem.at[u])
+        for u in range(3)
+    ] + [pltpu.make_async_copy(vecs, out_vecs.at[core, me], local_sem.at[3])]
+    for copy in local:
+        copy.start()
+    place.meet()
+    for copy in local:
+        copy.wait()
+    gathers = [
+        Gather(place, out_units.at[u, core], send_sem, recv_sem, COPIES * u) for u in range(3)
+    ]
+    small = Gather(place, out_vecs.at[core], send_sem, recv_sem, COPIES * 3)
+
+    def to_core(u, ref):
+        return pltpu.make_async_remote_copy(
+            src_ref=ref.at[core],
+            dst_ref=ref.at[core],
+            send_sem=core_send.at[u],
+            recv_sem=core_recv.at[u],
+            device_id=(me, 1 - core),
+            device_id_type=MESH,
+        )
+
+    across = []
+    for u, step in ORDER:
+        getattr(gathers[u], f"step{step}")()
+        if u == 0:
+            getattr(small, f"step{step}")()
+        if step == 3:
+            across.append(to_core(u, out_units.at[u]))
+            across[-1].start()
+            if u == 0:
+                across.append(to_core(3, out_vecs))
+                across[-1].start()
+    for each in gathers + [small]:
+        each.finish()
+    for copy in across:
+        copy.wait()
+
+
+def gather(units, vecs):
+    return pl.pallas_call(
+        gather_kernel,
+        out_shape=(
+            jax.ShapeDtypeStruct((3, 2, 16, 128, 1024), jnp.bfloat16),
+            jax.ShapeDtypeStruct((2, 16, 16, 128), jnp.bfloat16),
+        ),
+        in_specs=[pl.BlockSpec(memory_space=pltpu.VMEM)] * 2,
+        out_specs=(
+            pl.BlockSpec(memory_space=pltpu.HBM),
+            pl.BlockSpec(memory_space=pltpu.HBM),
+        ),
+        scratch_shapes=[
+            pltpu.SemaphoreType.DMA((4,)),
+            pltpu.SemaphoreType.DMA((4,)),
+            pltpu.SemaphoreType.DMA((4,)),
+            pltpu.SemaphoreType.DMA((4 * COPIES,)),
+            pltpu.SemaphoreType.DMA((4 * COPIES,)),
+        ],
+        compiler_params=pltpu.CompilerParams(
+            collective_id=0, has_side_effects=True, vmem_limit_bytes=56 << 20
+        ),
+    )(units, vecs)
+
+
+def reduce_kernel(
+    units,
+    vecs,
+    out_units,
+    out_vecs,
+    terms,
+    across,
+    vec_terms,
+    vec_across,
+    landed,
+    vec_landed,
+    local_sem,
+    core_send,
+    core_recv,
+    send_sem,
+    recv_sem,
+):
+    place = Place()
+    me, core = place.me, place.core
+    local = [
+        pltpu.make_async_copy(units.at[core, u], terms.at[u], local_sem.at[u]) for u in range(3)
+    ] + [pltpu.make_async_copy(vecs.at[core], vec_terms, local_sem.at[3])]
+    for copy in local:
+        copy.start()
+    place.meet()
+    swaps = []
+    for u in (2, 1, 0, 3):
+        source, target = (vecs.at[1 - core], vec_across) if u == 3 else (units.at[1 - core, u], across.at[u])
+        swaps.append(
+            pltpu.make_async_remote_copy(
+                src_ref=source,
+                dst_ref=target,
+                send_sem=core_send.at[u],
+                recv_sem=core_recv.at[u],
+                device_id=(me, 1 - core),
+                device_id_type=MESH,
+            )
+        )
+        swaps[-1].start()
+    for copy in local:
+        copy.wait()
+    reduces = [
+        Reduce(place, terms.at[u], landed.at[u], send_sem, recv_sem, COPIES * u) for u in range(3)
+    ]
+    small = Reduce(place, vec_terms, vec_landed, send_sem, recv_sem, COPIES * 3)
+    for n, step in ORDER:
+        u = 2 - n
+        if step == 0:
+            swaps[n].wait_recv()
+
+            @pl.loop(0, 16)
+            def _(i):
+                terms[u, i] += across[u, i]
+
+            if u == 0:
+                swaps[3].wait_recv()
+                vec_terms[...] += vec_across[...]
+        getattr(reduces[u], f"step{step}")()
+        if u == 0:
+            getattr(small, f"step{step}")()
+    for u in (2, 1, 0):
+        out_units[u] = reduces[u].result()
+    out_vecs[...] = small.result()
+    for each in reduces + [small]:
+        each.finish()
+    for copy in swaps:
+        copy.wait_send()
+
+
+def reduce(units, vecs):
+    return pl.pallas_call(
+        reduce_kernel,
+        out_shape=(
+            jax.ShapeDtypeStruct((3, 128, 1024), jnp.float32),
+            jax.ShapeDtypeStruct((8, 128), jnp.float32),
+        ),
+        in_specs=[pl.BlockSpec(memory_space=pltpu.HBM)] * 2,
+        out_specs=(
+            pl.BlockSpec(memory_space=pltpu.VMEM),
+            pl.BlockSpec(memory_space=pltpu.VMEM),
+        ),
+        scratch_shapes=[
+            pltpu.VMEM((3, 16, 128, 1024), jnp.bfloat16),
+            pltpu.VMEM((3, 16, 128, 1024), jnp.bfloat16),
+            pltpu.VMEM((16, 8, 128), jnp.float32),
+            pltpu.VMEM((16, 8, 128), jnp.float32),
+            pltpu.VMEM((3, COPIES, 128, 1024), jnp.bfloat16),
+            pltpu.VMEM((COPIES, 8, 128), jnp.float32),
+            pltpu.SemaphoreType.DMA((4,)),
+            pltpu.SemaphoreType.DMA((4,)),
+            pltpu.SemaphoreType.DMA((4,)),
+            pltpu.SemaphoreType.DMA((4 * COPIES,)),
+            pltpu.SemaphoreType.DMA((4 * COPIES,)),
+        ],
+        compiler_params=pltpu.CompilerParams(
+            collective_id=1, has_side_effects=True, vmem_limit_bytes=56 << 20
+        ),
+    )(units, vecs)
+
+
 HD = 64
-
-
 epsilon = 1e-12
 
+
+def pieces_of(vectors):
+    return jnp.concatenate(vectors).reshape(-1, 128)
+
+
+def fast_device(
+    tokens,
+    lengths,
+    cotangent,
+    query_weight,
+    key_weight,
+    value_weight,
+    output_weight,
+    query_bias,
+    value_bias,
+    output_bias,
+    first_gain,
+    first_shift,
+    inner_weight,
+    inner_bias,
+    outer_weight,
+    outer_bias,
+    second_gain,
+    second_shift,
+):
+    low = jnp.bfloat16
+    count, seq, width = tokens.shape
+    rows = count * seq
+    heads = width // HD
+    scale = 1.0 / math.sqrt(HD)
+    units = jnp.stack(
+        [
+            jnp.concatenate([query_weight, key_weight, value_weight, output_weight]).astype(low),
+            inner_weight.astype(low).reshape(128, 1024),
+            outer_weight.astype(low),
+        ]
+    )
+    short = (query_bias, value_bias, output_bias, first_gain, first_shift, outer_bias, second_gain, second_shift)
+    vecs = jnp.pad(jnp.concatenate(short + (inner_bias,)).astype(low).reshape(3, 128), ((0, 13), (0, 0)))
+    units, vecs = gather(units, vecs)
+    attn = units[0].transpose(1, 0, 2, 3).reshape(32, 4, 32, 1024).transpose(1, 0, 2, 3).reshape(4, 1024, 1024)
+    query_use, key_use, value_use, output_use = attn[0], attn[1], attn[2], attn[3]
+    inner_use = units[1].transpose(1, 0, 2, 3).reshape(1024, 4096)
+    outer_use = units[2].transpose(1, 0, 2, 3).reshape(4096, 1024)
+    flat = vecs.transpose(1, 0, 2, 3)[:, :, :3].reshape(32, 384).astype(jnp.float32)
+    full = flat[:, :256].reshape(32, 8, 32).transpose(1, 0, 2).reshape(8, 1024)
+    bias_query, bias_value, bias_output, gain_first, shift_first, bias_outer, gain_second, shift_second = [full[i] for i in range(8)]
+    bias_inner = flat[:, 256:].reshape(4096)
+
+    token_rows = tokens.reshape(rows, width)
+    cot_rows = cotangent.reshape(rows, width).astype(jnp.float32)
+    valid = jnp.arange(seq, dtype=jnp.int32)[None, :] < lengths[:, None]
+
+    def split(array):
+        return array.reshape(count, seq, heads, HD)
+
+    queries = split((matmul(token_rows, query_use) + bias_query).astype(low))
+    keys = split(matmul(token_rows, key_use).astype(low))
+    values = split((matmul(token_rows, value_use) + bias_value).astype(low))
+    scores = jnp.einsum("sqhd,skhd->shqk", queries, keys, preferred_element_type=jnp.float32) * scale
+    scores = jnp.where(valid[:, None, None, :], scores, -1000000000.0)
+    probs = jax.nn.softmax(scores, axis=-1)
+    probs_low = probs.astype(low)
+    mixed = (
+        jnp.einsum("shqk,skhd->sqhd", probs_low, values, preferred_element_type=jnp.float32)
+        .reshape(rows, width)
+        .astype(low)
+    )
+    residual = token_rows.astype(jnp.float32) + matmul(mixed, output_use) + bias_output
+    first, pull_first = jax.vjp(normalize, residual, gain_first, shift_first)
+    first_low = first.astype(low)
+    inner = matmul(first_low, inner_use) + bias_inner
+    active, pull_gelu = jax.vjp(gelu_exact, inner)
+    active = active.astype(low)
+    second_in = first + matmul(active, outer_use) + bias_outer
+    layer_rows, pull_second = jax.vjp(normalize, second_in, gain_second, shift_second)
+    d_second, d_gain_second, d_shift_second = pull_second(cot_rows)
+    d_outer = d_second.astype(low)
+    outer_grad = matmul_left_t(active, d_outer)
+    (d_inner,) = pull_gelu(matmul_right_t(d_outer, outer_use))
+    d_inner = d_inner.astype(low)
+    inner_grad = matmul_left_t(first_low, d_inner)
+    d_first = matmul_right_t(d_inner, inner_use) + d_second
+    d_residual, d_gain_first, d_shift_first = pull_first(d_first)
+    d_branch = d_residual.astype(low)
+    output_grad = matmul_left_t(mixed, d_branch)
+    d_mixed = split(matmul_right_t(d_branch, output_use).astype(low))
+    d_probs = jnp.einsum("sqhd,skhd->shqk", d_mixed, values, preferred_element_type=jnp.float32)
+    d_values = jnp.einsum("shqk,sqhd->skhd", probs_low, d_mixed, preferred_element_type=jnp.float32)
+    delta = jnp.sum(probs * d_probs, axis=-1, keepdims=True)
+    d_scores = (probs * (d_probs - delta)).astype(low)
+    d_queries = jnp.einsum("shqk,skhd->sqhd", d_scores, keys, preferred_element_type=jnp.float32) * scale
+    d_keys = jnp.einsum("shqk,sqhd->skhd", d_scores, queries, preferred_element_type=jnp.float32) * scale
+    d_queries, d_keys, d_values = [
+        each.reshape(rows, width).astype(low) for each in (d_queries, d_keys, d_values)
+    ]
+    token_grad = (
+        d_residual
+        + matmul_right_t(d_queries, query_use)
+        + matmul_right_t(d_keys, key_use)
+        + matmul_right_t(d_values, value_use)
+    )
+    attn_grad = [matmul_left_t(token_rows, each) for each in (d_queries, d_keys, d_values)] + [output_grad]
+    attn_grad = jnp.stack([each.astype(low) for each in attn_grad])
+
+    def by_core(grads):
+        return grads.reshape(16, 2, 128, 1024).transpose(1, 0, 2, 3)
+
+    units = jnp.stack(
+        [
+            by_core(attn_grad.reshape(4, 32, 32, 1024).transpose(1, 0, 2, 3)),
+            by_core(inner_grad.astype(low)),
+            by_core(outer_grad.astype(low)),
+        ],
+        axis=1,
+    )
+    vectors = jnp.stack(
+        [
+            row_sum(d_queries),
+            row_sum(d_values),
+            row_sum(d_branch),
+            d_gain_first,
+            d_shift_first,
+            row_sum(d_outer),
+            d_gain_second,
+            d_shift_second,
+        ]
+    )
+    flat = jnp.concatenate(
+        [vectors.reshape(8, 32, 32).transpose(1, 0, 2).reshape(32, 256), row_sum(d_inner).reshape(32, 128)], axis=1
+    )
+    vecs = jnp.pad(flat.reshape(16, 2, 3, 128).transpose(1, 0, 2, 3), ((0, 0), (0, 0), (0, 5), (0, 0)))
+    units, vecs = reduce(units, vecs)
+    flat = vecs[:3].reshape(384)
+    part = [flat[32 * i : 32 * i + 32] for i in range(8)]
+    return (
+        layer_rows.astype(low).reshape(count, seq, width),
+        token_grad.astype(low).reshape(count, seq, width),
+        units[0, 0:32],
+        units[0, 32:64],
+        units[0, 64:96],
+        units[0, 96:128],
+        part[0],
+        part[1],
+        part[2],
+        part[3],
+        part[4],
+        units[1].reshape(32, 4096),
+        flat[256:384],
+        units[2],
+        part[5],
+        part[6],
+        part[7],
+    )
 
 def normalize(hidden, gain, shift):
     center = hidden - jnp.mean(hidden, axis=-1, keepdims=True)
@@ -325,6 +853,8 @@
         P(("dp", "fsdp")),
         P(("dp", "fsdp")),
     )
+    dims = dict(mesh.shape)
+    device = fast_device if dims == {"dp": 16, "fsdp": 2} else per_device
     return jax.shard_map(
-        per_device, mesh=mesh, in_specs=in_specs, out_specs=out_specs, check_vma=False
-    )
+        device, mesh=mesh, in_specs=in_specs, out_specs=out_specs, check_vma=False
+    )

time: 1450 us -> 545 us (0.38)
  waiting for transfers between devices: 1040 us -> 0 us
  Pallas kernels: 0 us -> 233 us
  blocking collectives: 123 us -> 0 us
  local copies, waits for them, and re-layouts: 50.5 us -> 134 us
  matrix products: 178 us -> 124 us
    reduce_scatter x3 -> x0, waiting for transfers between devices: 508 us -> none  [the longest x1 187 us: per_device(): lax.psum_scatter(ffn_totals[2], ('dp', 'fsdp'), scatter_dimension=0, tile...]
    unnamed x15 -> x0, waiting for transfers between devices: 294 us -> none
    all_gather x6 -> x0, waiting for transfers between devices: 235 us -> none  [the longest x1 68.7 us: per_device(): lax.all_gather(ffn_half[0], ('dp', 'fsdp'), axis=0, tiled=True)]
    pallas_call x0 -> x2, Pallas kernels: none -> 233 us  [the longest x1 122 us: reduce(): pl.pallas_call(reduce_kernel, out_shape=(jax.ShapeDtypeStruct((3, 128, 10...]
    unnamed x2 -> x0, blocking collectives: 82.9 us -> none
    reshape x0 -> x15, local copies, waits for them, and re-layouts: none -> 63.7 us  [the longest x4 38.6 us: by_core(): return grads.reshape(16, 2, 128, 1024).transpose(1, 0, 2, 3)]
    transpose x0 -> x4, local copies, waits for them, and re-layouts: none -> 41.7 us  [the longest x2 25.1 us: fast_device(): outer_use = units[2].transpose(1, 0, 2, 3).reshape(4096, 1024)]
    all_gather x1 -> x0, blocking collectives: 40.4 us -> none  [per_device(): lax.all_gather(ffn_half[1], ('dp', 'fsdp'), axis=0, tiled=True)]
  transfers between devices with their start and end apart: 12 -> 0, of which waited for: 11 -> 0; matrix products, arithmetic and copies ran while one was open for 10% -> 0% of each run, Pallas kernels for 0% -> 0%
where the time goes in v1:
time: 545 us; the launch traced here: 535 us
  Pallas kernels  233 us (43%)
  local copies, waits for them, and re-layouts  134 us (25%)
  matrix products  124 us (23%)
  other arithmetic  42.1 us (8%)
    pallas_call x1, Pallas kernels, reduce(): pl.pallas_call(reduce_kernel, out_shape=(jax.ShapeDtypeStruct((3, 128, 10...  122 us
    pallas_call x1, Pallas kernels, gather(): pl.pallas_call(gather_kernel, out_shape=(jax.ShapeDtypeStruct((3, 2, 16,...  111 us
    dot_general x6, matrix products, matmul(): return jnp.dot(left, right, preferred_element_type=jnp.float32)  48.6 us
    reshape x4, local copies, waits for them, and re-layouts, by_core(): return grads.reshape(16, 2, 128, 1024).transpose(1, 0, 2, 3)  38.6 us
    dot_general x6, matrix products, matmul_right_t(): lax.dot_general(left, right, (((1,), (1,)), ((), ())), preferred_element_...  31.6 us
    transpose x2, local copies, waits for them, and re-layouts, fast_device(): outer_use = units[2].transpose(1, 0, 2, 3).reshape(4096, 1024)  25.1 us
    dot_general x6, matrix products, matmul_left_t(): lax.dot_general(left, right, (((0,), (0,)), ((), ())), preferred_element_...  22.8 us
    another operation x1, other arithmetic, fast_device(): jnp.stack([by_core(attn_grad.reshape(4, 32, 32, 1024).transpose(1, 0, 2,...  17.2 us

profile of v1, /device:TPU:0, one launch (start us, length us, event | category | flops | bytes accessed | tf_op | source)
XLA Modules:
  0.0 535.3 jit_solution(13239052338731759604)
XLA Ops:
  0.7 1.0 convert_bitcast_fusion.1
  1.8 1.0 convert_bitcast_fusion.3
  2.8 1.1 convert_element_type.177
  4.0 1.1 convert_bitcast_fusion
  5.1 0.9 pad_maximum_fusion.2.units
  6.9 110.6 %shard_map.305 = (bf16[3,2,16,128,1024]{4,3,2,1,0:T(8,128)(2,1)}, bf16[2,16,16,128]{3,2,1,0:T(8,128)(2,1)}) custom-call(bf16[3,128,1024]{2,1,0:T(8,128)(2,1)} %pad_maximum_fusion.2.units, bf16[16,128]{1,0:T(8,128)(2,1)} %pad.8.vecs), custom_call_target="tpu_custom_call" | custom-call | tf_op jit(solution)/shard_map/pallas_call | solution.py:260
  117.5 0.9 slice_convert_fusion
  119.0 16.8 %slice_bitcast_fusion = (bf16[16,2,128,1024]{3,2,0,1:T(8,128)(2,1)}, bf16[16,2,128,1024]{3,2,0,1:T(8,128)(2,1)}, bf16[16,2,128,1024]{3,2,0,1:T(8,128)(2,1)}) fusion(bf16[3,2,16,128,1024]{4,3,2,1,0:T(8,128)(2,1)} %get-tuple-element.21), kind=kLoop, calls=%fused_computation.12 | loop fusion | bytes 50331648 | tf_op jit(solution)/shard_map/transpose | solution.py:430
  135.7 8.2 %copy.76 = bf16[16,2,128,1024]{3,2,1,0:T(8,128)(2,1)} copy(bf16[16,2,128,1024]{3,2,0,1:T(8,128)(2,1)} %get-tuple-element.52) | data formatting | bytes 16777216 | tf_op jit(solution)/shard_map/transpose | solution.py:427
  143.9 5.5 %fusion.55 = (bf16[1,32,32,1024]{3,2,0,1:T(8,128)(2,1)}, bf16[1,32,32,1024]{3,2,0,1:T(8,128)(2,1)S(1)}, bf16[1,32,32,1024]{3,2,0,1:T(8,128)(2,1)S(1)}, bf16[1,32,32,1024]{3,2,0,1:T(8,128)(2,1)}) fusion(bf16[4,32,32,1024]{3,2,0,1:T(8,128)(2,1)} %bitcast.193), kind=kLoop, calls=%fused_computation.137 | loop fusion | bytes 16777216 | tf_op jit(solution)/shard_map/slice | solution.py:428
  149.5 1.3 copy-done.19
  150.8 2.3 fusion.34
  153.1 1.3 reshape.310
  154.5 3.9 fusion.26
  158.3 1.3 reshape.311
  159.7 1.3 fusion.41
  161.1 5.5 %fusion.57 = (f32[2,16,256]{2,1,0:T(8,128)S(1)}, f32[2,16,256,256]{2,3,1,0:T(8,128)}) fusion(f32[2,16,256,256]{2,3,1,0:T(8,128)S(1)} %fusion.41, pred[2,256]{1,0:T(4,128)(4,1)S(1)} %iota_compare_fusion), kind=kOutput, calls=%fused_computation.139 | output fusion | flops 12583167 | bytes 16810496 | tf_op jit(solution)/shard_map/sub | solution.py:448
  166.7 2.5 fusion.33
  169.8 4.6 fusion.30
  174.3 1.1 copy.82
  175.8 3.5 fusion.58
  179.8 8.4 %copy.83 = bf16[16,2,128,1024]{3,2,1,0:T(8,128)(2,1)} copy(bf16[16,2,128,1024]{3,2,0,1:T(8,128)(2,1)} %get-tuple-element.51) | data formatting | bytes 16777216 | tf_op jit(solution)/shard_map/transpose | solution.py:429
  188.2 14.0 %reshape.312 = bf16[1024,4096]{1,0:T(8,128)(2,1)} reshape(bf16[16,2,128,1024]{3,2,1,0:T(8,128)(2,1)} %copy.83) | data formatting | bytes 16777216 | tf_op jit(solution)/shard_map/reshape | solution.py:429
  202.2 27.5 %multiply_convert_fusion.1 = (bf16[512,4096]{1,0:T(8,128)(2,1)}, f32[512,4096]{1,0:T(8,128)}, f32[512,4096]{1,0:T(8,128)}) fusion(f32[4096]{0:T(1024)S(1)} %slice_bitcast_fusion.8, bf16[1024,4096]{1,0:T(8,128)(2,1)} %reshape.312, f32[512,1024]{1,0:T(8,128)S(1)} %get-tuple-element.75, f32[1024]{0:T(1024)S(1)} %add.125, f32[1024]{0:T(1024)S(1)} %mul.165, ...), kind=kOutput, calls=%fused_computation.13 | convolution fusion | flops 4436000768 | bytes 31485952 | tf_op jit(solution)/shard_map/dot_general | solution.py:553
  229.7 8.3 %copy.84 = bf16[16,2,128,1024]{3,2,1,0:T(8,128)(2,1)} copy(bf16[16,2,128,1024]{3,2,0,1:T(8,128)(2,1)} %get-tuple-element.50) | data formatting | bytes 16777216 | tf_op jit(solution)/shard_map/transpose | solution.py:430
  238.0 8.9 %fusion.59 = (f32[512]{0:T(512)S(1)}, f32[512,1024]{1,0:T(8,128)S(1)}) fusion(f32[1024]{0:T(1024)S(1)} %add.132, bf16[512,4096]{1,0:T(8,128)(2,1)} %get-tuple-element.48, bf16[4096,1024]{1,0:T(8,128)(2,1)} %bitcast.198, f32[1024]{0:T(1024)S(1)} %add.125, f32[1024]{0:T(1024)S(1)} %mul.165, f32[512]{0:T(512)S(1)} %fusion.45, f32[512,1024]{1,0:T(8,128)S(1)} %copy-done.3, ...), kind=kOutput, calls=%fused_computation.141 | convolution fusion | flops 4298636800 | bytes 16795648 | tf_op jit(solution)/shard_map/dot_general | solution.py:553
  247.4 0.8 fusion.14
  248.3 1.9 fusion.53
  250.5 13.7 %convert_reduce_fusion = (f32[4096]{0:T(1024)S(1)}, bf16[512,4096]{1,0:T(8,128)(2,1)S(1)}) fusion(f32[512,4096]{1,0:T(8,128)} %get-tuple-element.49, f32[512,4096]{1,0:T(8,128)} %get-tuple-element.76, f32[4096]{0:T(1024)S(1)} %slice_bitcast_fusion.8, bf16[512,1024]{1,0:T(8,128)(2,1)S(1)} %get-tuple-element.39, bf16[4096,1024]{1,0:T(8,128)(2,1)} %bitcast.199), kind=kOutput, calls=%fused_computation.8 | convolution fusion | flops 4330614784 | bytes 30441472 | tf_op jit(solution)/shard_map/dot_general | solution.py:563
  264.3 9.1 %multiply_reduce_fusion.1 = (f32[1024]{0:T(1024)S(1)}, f32[512]{0:T(512)S(1)}, f32[1024]{0:T(1024)S(1)}, f32[512,1024]{1,0:T(8,128)S(1)}) fusion(f32[512,1024]{1,0:T(8,128)S(1)} %copy-done.4, f32[512]{0:T(512)S(1)} %fusion.45, f32[512]{0:T(512)S(1)} %broadcast_multiply_fusion.1, f32[1024]{0:T(1024)S(1)} %mul.165, f32[512,1024]{1,0:T(8,128)S(1)} %get-tuple-element.47, ...), kind=kOutput, calls=%fused_computation.48 | convolution fusion | flops 4300207616 | bytes 18894848 | tf_op jit(solution)/shard_map/dot_general | solution.py:563
  274.1 1.3 copy-done.10
  275.7 1.0 copy-done.27
  276.6 2.3 convolution_convert_fusion.6
  278.9 4.2 reshape.326
  283.1 3.5 copy.86
  286.6 6.2 %convert_reduce_fusion.4 = (f32[16,64]{1,0:T(8,128)S(1)}, bf16[2,256,16,64]{1,3,2,0:T(8,128)(2,1)}) fusion(bf16[2,256,16,64]{1,3,2,0:T(8,128)(2,1)} %copy.86, f32[2,16,256,256]{2,3,1,0:T(8,128)} %get-tuple-element.73, f32[2,16,256]{2,1,0:T(8,128)S(1)} %get-tuple-element.72), kind=kOutput, calls=%fused_computation.50 | convolution fusion | flops 274201600 | bytes 10522624 | tf_op jit(solution)/shard_map/shqk,sqhd->skhd/dot_general | solution.py:475
  292.9 5.5 %multiply_reduce_fusion = (f32[2,16,256]{2,1,0:T(8,128)S(1)}, f32[2,16,256,256]{2,3,1,0:T(8,128)S(1)}) fusion(f32[2,16,256,256]{2,3,1,0:T(8,128)} %get-tuple-element.73, f32[2,16,256]{2,1,0:T(8,128)S(1)} %get-tuple-element.72, bf16[2,256,16,64]{1,3,2,0:T(8,128)(2,1)} %copy.86, bf16[2,256,16,64]{1,0,3,2:T(2,128)(2,1)} %copy-done.23), kind=kOutput, calls=%fused_computation.10 | convolution fusion | flops 274718720 | bytes 18939904 | tf_op jit(solution)/shard_map/sqhd,skhd->shqk/dot_general | solution.py:474
  298.4 4.4 multiply_convert_fusion
  302.8 1.9 copy-done
  304.7 1.8 convert_reduce_fusion.5
  308.4 2.9 convolution_convert_fusion.2
  311.3 1.1 copy.96
  312.6 1.3 convolution_convert_fusion.3
  314.2 1.1 copy.90
  315.6 1.3 convolution_convert_fusion.5
  316.9 1.2 copy-done.1
  318.4 1.4 fusion.36
  319.8 1.1 copy.93
  321.2 1.3 convolution_convert_fusion.4
  322.5 4.1 pad_maximum_fusion.1
  326.5 8.2 %copy.139 = bf16[16,2,128,1024]{3,2,0,1:T(8,128)(2,1)} copy(bf16[16,2,128,1024]{3,2,1,0:T(8,128)(2,1)} %bitcast.194) | data formatting | bytes 16777216 | tf_op jit(solution)/shard_map/reshape | solution.py:493
  334.7 9.2 %convolution_convert_fusion.1 = bf16[1024,4096]{1,0:T(8,128)(2,1)} fusion(bf16[512,4096]{1,0:T(8,128)(2,1)} %copy-done.45, f32[512,1024]{1,0:T(8,128)S(1)} %copy-done.4, f32[1024]{0:T(1024)S(1)} %add.125, f32[1024]{0:T(1024)S(1)} %mul.165, f32[512]{0:T(512)S(1)} %fusion.45, f32[512]{0:T(512)S(1)} %broadcast_multiply_fusion.1), kind=kOutput, calls=%fused_computation.32 | convolution fusion | flops 4301783040 | bytes 14692352 | tf_op jit(solution)/shard_map/dot_general | solution.py:557
  343.9 14.0 %reshape.318 = bf16[16,2,128,1024]{3,2,1,0:T(8,128)(2,1)} reshape(bf16[1024,4096]{1,0:T(8,128)(2,1)} %convolution_convert_fusion.1) | data formatting | bytes 16777216 | tf_op jit(solution)/shard_map/reshape | solution.py:493
  357.9 8.3 %copy.138 = bf16[16,2,128,1024]{3,2,0,1:T(8,128)(2,1)} copy(bf16[16,2,128,1024]{3,2,1,0:T(8,128)(2,1)} %reshape.318) | data formatting | bytes 16777216 | tf_op jit(solution)/shard_map/reshape | solution.py:493
  366.2 6.8 %convolution_convert_fusion = bf16[4096,1024]{1,0:T(8,128)(2,1)} fusion(bf16[512,4096]{1,0:T(8,128)(2,1)S(1)} %copy-done.44, bf16[512,1024]{1,0:T(8,128)(2,1)S(1)} %copy-done.22), kind=kOutput, calls=%fused_computation.31 | convolution fusion | flops 4299161600 | bytes 13631488 | tf_op jit(solution)/shard_map/dot_general | solution.py:557
  373.0 8.2 %copy.137 = bf16[16,2,128,1024]{3,2,0,1:T(8,128)(2,1)} copy(bf16[16,2,128,1024]{3,2,1,0:T(8,128)(2,1)} %bitcast.200) | data formatting | bytes 16777216 | tf_op jit(solution)/shard_map/reshape | solution.py:493
  381.1 17.2 %pad_maximum_fusion.units = bf16[2,3,16,128,1024]{4,3,2,1,0:T(8,128)(2,1)} fusion(bf16[2,1,16,128,1024]{4,3,2,1,0:T(8,128)(2,1)} %bitcast.197, bf16[2,1,16,128,1024]{4,3,2,1,0:T(8,128)(2,1)} %bitcast.196, bf16[2,1,16,128,1024]{4,3,2,1,0:T(8,128)(2,1)} %bitcast.195), kind=kLoop, calls=%fused_computation.1 | loop fusion | flops 25165824 | bytes 50331648 | tf_op jit(solution)/shard_map/stack | solution.py:495
  398.4 122.4 %shard_map.306 = (f32[3,128,1024]{2,1,0:T(8,128)}, f32[8,128]{1,0:T(8,128)}) custom-call(bf16[2,3,16,128,1024]{4,3,2,1,0:T(8,128)(2,1)} %pad_maximum_fusion.units, f32[2,16,8,128]{3,2,1,0:T(8,128)} %pad.9.vecs), custom_call_target="tpu_custom_call" | custom-call | tf_op jit(solution)/shard_map/pallas_call | solution.py:354
  520.8 2.2 slice_bitcast_fusion.3
  523.1 1.0 reshape_squeeze.3
  524.1 1.9 slice_bitcast_fusion.4
  527.1 2.7 fusion.60
  529.9 1.3 fusion.61
  532.3 2.5 add_convert_fusion.1
  (150 shorter events, 10.3 us)
Async XLA Ops:
  0.7 5.4 %copy-start.34 = (f32[32]{0:T(128)S(1)}, f32[32]{0:T(128)}, u32[]{:S(2)}) copy-start(f32[32]{0:T(128)} %param.25) | copy-start | bytes 388
  0.7 5.4 %copy-start.35 = (f32[32]{0:T(128)S(1)}, f32[32]{0:T(128)}, u32[]{:S(2)}) copy-start(f32[32]{0:T(128)} %param.26) | copy-start | bytes 388
  0.7 5.4 %copy-start.36 = (f32[32]{0:T(128)S(1)}, f32[32]{0:T(128)}, u32[]{:S(2)}) copy-start(f32[32]{0:T(128)} %param.27) | copy-start | bytes 388
  0.7 5.4 %copy-start.37 = (f32[32]{0:T(128)S(1)}, f32[32]{0:T(128)}, u32[]{:S(2)}) copy-start(f32[32]{0:T(128)} %param.28) | copy-start | bytes 388
  0.7 5.4 %copy-start.38 = (f32[32]{0:T(128)S(1)}, f32[32]{0:T(128)}, u32[]{:S(2)}) copy-start(f32[32]{0:T(128)} %param.29) | copy-start | bytes 388
  0.7 5.4 %copy-start.39 = (f32[32]{0:T(128)S(1)}, f32[32]{0:T(128)}, u32[]{:S(2)}) copy-start(f32[32]{0:T(128)} %param.33) | copy-start | bytes 388
  0.7 5.4 %copy-start.40 = (f32[32]{0:T(128)S(1)}, f32[32]{0:T(128)}, u32[]{:S(2)}) copy-start(f32[32]{0:T(128)} %param.34) | copy-start | bytes 388
  0.7 5.4 %copy-start.41 = (f32[32]{0:T(128)S(1)}, f32[32]{0:T(128)}, u32[]{:S(2)}) copy-start(f32[32]{0:T(128)} %param.35) | copy-start | bytes 388
  0.7 5.4 %copy-start.42 = (f32[128]{0:T(128)S(1)}, f32[128]{0:T(128)}, u32[]{:S(2)}) copy-start(f32[128]{0:T(128)} %param.31) | copy-start | bytes 1540
  143.9 6.9 %copy-start.31 = (bf16[2,256,1024]{2,1,0:T(8,128)(2,1)S(1)}, bf16[2,256,1024]{2,1,0:T(8,128)(2,1)}, u32[]{:S(2)}) copy-start(bf16[2,256,1024]{2,1,0:T(8,128)(2,1)} %param.18) | copy-start | bytes 3145732
  149.5 1.3 copy-start.19
  149.5 5.0 copy-start.17
  154.4 5.2 copy-start.5
  159.7 1.3 copy-start.7
  159.7 1.3 copy-start.43
  161.1 5.6 %copy-start.15 = (bf16[1,32,32,1024]{3,2,0,1:T(8,128)(2,1)S(1)}, bf16[1,32,32,1024]{3,2,0,1:T(8,128)(2,1)}, u32[]{:S(2)}) copy-start(bf16[1,32,32,1024]{3,2,0,1:T(8,128)(2,1)} %get-tuple-element.56) | copy-start | bytes 6291460
  169.8 4.6 copy-start.23
  175.7 4.0 copy-start.13
  179.3 22.9 %copy-start.2 = (f32[512,1024]{1,0:T(8,128)}, f32[512,1024]{1,0:T(8,128)S(1)}, u32[]{:S(2)}) copy-start(f32[512,1024]{1,0:T(8,128)S(1)} %get-tuple-element.75) | copy-start | bytes 6291460
  229.7 8.3 %copy-start.3 = (f32[512,1024]{1,0:T(8,128)S(1)}, f32[512,1024]{1,0:T(8,128)}, u32[]{:S(2)}) copy-start(f32[512,1024]{1,0:T(8,128)} %copy-done.2) | copy-start | bytes 6291460
  238.0 9.4 %copy-start.9 = (bf16[2,256,1024]{2,1,0:T(8,128)(2,1)S(1)}, bf16[2,256,1024]{2,1,0:T(8,128)(2,1)}, u32[]{:S(2)}) copy-start(bf16[2,256,1024]{2,1,0:T(8,128)(2,1)} %param.20) | copy-start | bytes 3145732
  250.5 13.8 %copy-start.21 = (bf16[512,1024]{1,0:T(8,128)(2,1)}, bf16[512,1024]{1,0:T(8,128)(2,1)S(1)}, u32[]{:S(2)}) copy-start(bf16[512,1024]{1,0:T(8,128)(2,1)S(1)} %get-tuple-element.39) | copy-start | bytes 3145732
  250.5 13.8 %copy-start.4 = (f32[512,1024]{1,0:T(8,128)S(1)}, f32[512,1024]{1,0:T(8,128)}, u32[]{:S(2)}) copy-start(f32[512,1024]{1,0:T(8,128)} %copy-done.2) | copy-start | bytes 6291460
  264.2 9.1 %copy-start.45 = (bf16[512,4096]{1,0:T(8,128)(2,1)}, bf16[512,4096]{1,0:T(8,128)(2,1)S(1)}, u32[]{:S(2)}) copy-start(bf16[512,4096]{1,0:T(8,128)(2,1)S(1)} %get-tuple-element.43) | copy-start | bytes 12582916
  273.4 3.2 copy-start.12
  274.1 1.3 copy-start.10
  275.6 1.0 copy-start.27
  298.4 6.3 %copy-start.8 = (bf16[2,256,16,64]{1,0,3,2:T(2,128)(2,1)S(1)}, bf16[2,256,16,64]{1,0,3,2:T(2,128)(2,1)}, u32[]{:S(2)}) copy-start(bf16[2,256,16,64]{1,0,3,2:T(2,128)(2,1)} %copy-done.7) | copy-start | bytes 3145732
  302.8 1.9 copy-start
  308.4 2.9 copy-start.30
  311.2 1.4 copy-start.32
  312.6 1.3 copy-start.24
  312.6 1.6 copy-start.14
  315.6 1.3 copy-start.26
  315.6 2.6 copy-start.1
  315.6 2.9 copy-start.6
  321.2 1.3 copy-start.28
  357.9 8.3 %copy-start.22 = (bf16[512,1024]{1,0:T(8,128)(2,1)S(1)}, bf16[512,1024]{1,0:T(8,128)(2,1)}, u32[]{:S(2)}) copy-start(bf16[512,1024]{1,0:T(8,128)(2,1)} %copy-done.21) | copy-start | bytes 3145732
  357.9 8.3 %copy-start.44 = (bf16[512,4096]{1,0:T(8,128)(2,1)S(1)}, bf16[512,4096]{1,0:T(8,128)(2,1)}, u32[]{:S(2)}) copy-start(bf16[512,4096]{1,0:T(8,128)(2,1)} %get-tuple-element.48) | copy-start | bytes 12582916
  520.8 5.2 copy-start.33
  520.8 6.3 %copy-start.20 = (bf16[1,32,32,1024]{3,2,0,1:T(8,128)(2,1)S(1)}, bf16[1,32,32,1024]{3,2,0,1:T(8,128)(2,1)}, u32[]{:S(2)}) copy-start(bf16[1,32,32,1024]{3,2,0,1:T(8,128)(2,1)} %copy-done.19) | copy-start | bytes 6291460
  527.1 2.7 copy-start.18
  527.1 2.7 copy-start.29
  529.8 1.6 copy-start.11
  529.8 2.2 copy-start.16
  529.8 2.5 copy-start.25
